TPU v7x, 512 devices: a whole 4x4x16 slice. The times are simulated.
512 devices in a mesh: sector: 64 (over x, z), term: 8 (over y, core).
Axes of the slice: x: 4, y: 4, z: 16, core: 2. Of those that a mesh axis runs over, the one named last changes fastest.
Arguments:
- wavefunction: bfloat16 [8192, 8192], P('sector'), may hold values from -6 to 6
- left_env: bfloat16 [8, 64, 128, 128], P('term', 'sector'), may hold values from -0.1875 to 0.1875
- right_env: bfloat16 [8, 64, 128, 128], P('term', 'sector'), may hold values from -0.5 to 0.5
- left_sizes: int32 [64], replicated, may hold values from 1 to 128, 6144 in all
- right_sizes: int32 [64], replicated, may hold values from 1 to 128, 6144 in all
- charge_left: int32 [64], replicated, may hold values from 0 to 3
- charge_right: int32 [64], replicated, may hold values from 0 to 3
- term_shift: int32 [8], P('term'), may hold values from -1 to 1
Outputs:
- product: bfloat16 [8192, 8192], P('sector', 'term')
Inputs may be any that keep to these rules, and one draw needn't show every extreme that they name: `left_sizes`: some left block holds all 128 states; the sizes sum to 6144. `right_sizes`: some right block holds all 128 states; the sizes sum to 6144.
All inputs are finite; a program needn't handle non-finite values.
Results may differ from a plain program's by a relative error of at most 0.019.
Values may be sent and summed in bfloat16 or wider, within the bound.
A program may use at most 64 MiB of HBM per device.

v0:
```python
import jax
import jax.numpy as jnp
from jax import lax
from jax.sharding import PartitionSpec as P


def shifted(value, axis, steps):
    count = lax.axis_size(axis)
    initial, last = (max(0, -steps), min(count, count - steps))
    return lax.ppermute(value, axis, [(source, source + steps) for source in range(initial, last)])


def local(
    wavefunction,
    left_env,
    right_env,
    left_sizes,
    right_sizes,
    charge_left,
    charge_right,
    term_shift,
):
    block = left_env.shape[2]
    own_sector = lax.axis_index("sector")
    place = jnp.arange(block, dtype=jnp.int32)
    row_ok = place < left_sizes[own_sector]
    col_ok = (place[None, :] < right_sizes[:, None]).reshape(-1)
    pair_ok = jnp.repeat(jnp.abs(charge_left[own_sector] - charge_right) <= 1, block)
    allowed = (row_ok[:, None] & (pair_ok & col_ok)[None, :]).astype(jnp.bfloat16)
    masked = wavefunction * allowed
    piece = lax.all_gather(right_env, "sector", axis=1, tiled=True)
    count = piece.shape[1]
    columns = masked
    columns = columns.reshape(block, count, block)
    inner_part = jnp.einsum("ibj,tbkj->tibk", columns, piece, preferred_element_type=jnp.float32)
    inner = inner_part.reshape(piece.shape[0], block, count * block).astype(jnp.bfloat16)
    left_blocks = left_env[:, 0]
    zero_b = jnp.zeros((), jnp.bfloat16)
    left_stay = jnp.where((term_shift == 0)[:, None, None], left_blocks, zero_b)
    left_rise = jnp.where((term_shift == 1)[:, None, None], left_blocks, zero_b)
    left_fall = jnp.where((term_shift == -1)[:, None, None], left_blocks, zero_b)
    stay = jnp.einsum("tki,tim->km", left_stay, inner, preferred_element_type=jnp.float32)
    rise = jnp.einsum("tki,tim->km", left_rise, inner, preferred_element_type=jnp.float32).astype(
        jnp.bfloat16
    )
    fall = jnp.einsum("tki,tim->km", left_fall, inner, preferred_element_type=jnp.float32).astype(
        jnp.bfloat16
    )
    from_below = shifted(rise, "sector", 1)
    from_above = shifted(fall, "sector", -1)
    partial_sum = stay + from_below.astype(jnp.float32) + from_above.astype(jnp.float32)
    summed = lax.psum_scatter(
        partial_sum.astype(jnp.bfloat16), "term", scatter_dimension=1, tiled=True
    ).astype(jnp.float32)
    slice_width = summed.shape[1]
    column_start = lax.axis_index("term") * slice_width
    own_allowed = lax.dynamic_slice_in_dim(allowed, column_start, slice_width, 1)
    return (summed * own_allowed.astype(jnp.float32)).astype(jnp.bfloat16)


def solution(mesh):
    placed = (
        P("sector", None),
        P("term", "sector", None, None),
        P("term", "sector", None, None),
        P(),
        P(),
        P(),
        P(),
        P("term"),
    )
    return jax.shard_map(
        local, mesh=mesh, in_specs=placed, out_specs=P("sector", "term"), check_vma=False
    )
```

profile of v0, /device:TPU:1, one launch (start us, length us, event | category | flops | bytes accessed | tf_op | source)
XLA Modules:
  0.0 250.8 jit_solution(10334423336700343546)
XLA Ops:
  6.5 0.0 all-gather.2.cloned.1.call-start
  6.5 0.7 all-gather.2.cloned.1.call-update
  7.3 0.0 reduce-scatter.2.cloned.1.call-start
  7.3 1.2 dynamic_slice.10
  8.6 1.3 dynamic_slice.9
  10.5 0.6 iota_compare_fusion.1
  11.2 1.3 abs_compare_fusion
  12.5 0.7 fusion.19
  13.2 0.0 copy-start
  13.2 134.5 %all-gather.2.cloned.1.call-done = bf16[1,64,128,128]{3,2,0,1:T(8,128)(2,1)} async-done(((bf16[1,1,128,128]{3,2,0,1:T(8,128)(2,1)}), bf16[1,64,128,128]{3,2,0,1:T(8,128)(2,1)}) %all-gather.2.cloned.1.call-update) | async-done | bytes 2097168 | tf_op jit(solution)/shard_map/all_gather | solution.py:31
  147.7 3.9 %fusion.4 = bf16[64,128,128]{1,2,0:T(8,128)(2,1)S(1)} fusion(bf16[1,64,128,128]{3,2,0,1:T(8,128)(2,1)} %all-gather.2.cloned.1.call-done, bf16[128,8192]{1,0:T(8,128)(2,1)} %param.8, pred[8192]{0:T(1024)(128)(4,1)S(1)} %fusion.19, pred[128]{0:T(512)(128)(4,1)S(1)} %iota_compare_fusion.1), kind=kOutput, calls=%fused_computation.9 | convolution fusion | flops 271581184 | bytes 6299776 | tf_op jit(solution)/shard_map/ibj,tbkj->tibk/dot_general | solution.py:35
  151.6 0.0 copy-done
  151.6 0.7 convolution_convert_fusion.1
  152.3 2.7 %collective-permute-start = (bf16[128,8192]{1,0:T(8,128)(2,1)S(1)}, bf16[128,8192]{1,0:T(8,128)(2,1)S(1)}, u32[]{:S(2)}, u32[]{:S(2)}) collective-permute-start(bf16[128,8192]{1,0:T(8,128)(2,1)S(1)} %convolution_convert_fusion.1), channel_id=1, source_target_pairs={{0,8},{8,16},{16,24},{24,32},{32,40},{40,48},{48,56},{56,64},{64,7... | collective-permute-start | bytes 6291464 | tf_op jit(solution)/shard_map/ppermute | solution.py:10
  155.0 0.7 convolution_convert_fusion
  155.7 1.3 collective-permute-start.1
  157.0 32.5 %collective-permute-done = bf16[128,8192]{1,0:T(8,128)(2,1)S(1)} collective-permute-done((bf16[128,8192]{1,0:T(8,128)(2,1)S(1)}, bf16[128,8192]{1,0:T(8,128)(2,1)S(1)}, u32[]{:S(2)}, u32[]{:S(2)}) %collective-permute-start) | collective-permute-done | bytes 2097184 | tf_op jit(solution)/shard_map/ppermute | solution.py:10
  189.6 4.7 %collective-permute-done.1 = bf16[128,8192]{1,0:T(8,128)(2,1)S(1)} collective-permute-done((bf16[128,8192]{1,0:T(8,128)(2,1)S(1)}, bf16[128,8192]{1,0:T(8,128)(2,1)S(1)}, u32[]{:S(2)}, u32[]{:S(2)}) %collective-permute-start.1) | collective-permute-done | bytes 2097184 | tf_op jit(solution)/shard_map/ppermute | solution.py:10
  194.2 2.2 add_convert_fusion
  196.5 0.0 reduce-scatter.2.cloned.1.call-update
  196.5 0.6 broadcast_and_fusion
  197.1 45.1 %reduce-scatter.2.cloned.1.call-done = bf16[128,1024]{1,0:T(8,128)(2,1)} async-done(((bf16[128,8192]{1,0:T(8,128)(2,1)}), bf16[128,1024]{1,0:T(8,128)(2,1)}) %reduce-scatter.2.cloned.1.call-update) | async-done | bytes 262160 | tf_op jit(solution)/shard_map/reduce_scatter | solution.py:52
  242.3 1.7 multiply_convert_fusion
Async XLA Ops:
  6.5 141.2 %all-gather.2.cloned.1.call-start = ((), (), s32[]{:S(2)}) async-start(), calls=%async_computation.1 | async-start | bytes 2129920 | tf_op jit(solution)/shard_map/all_gather | solution.py:31
  7.3 235.0 %reduce-scatter.2.cloned.1.call-start = ((), (), s32[]{:S(2)}) async-start(), calls=%async_computation.2 | async-start | bytes 2359296 | tf_op jit(solution)/shard_map/reduce_scatter | solution.py:52
  13.2 138.4 %copy-start = (bf16[1,1,128,128]{3,2,1,0:T(8,128)(2,1)S(1)}, bf16[1,1,128,128]{3,2,1,0:T(8,128)(2,1)}, u32[]{:S(2)}) copy-start(bf16[1,1,128,128]{3,2,1,0:T(8,128)(2,1)} %param.9) | copy-start | bytes 98308
  152.3 37.3 %collective-permute-start = (bf16[128,8192]{1,0:T(8,128)(2,1)S(1)}, bf16[128,8192]{1,0:T(8,128)(2,1)S(1)}, u32[]{:S(2)}, u32[]{:S(2)}) collective-permute-start(bf16[128,8192]{1,0:T(8,128)(2,1)S(1)} %convolution_convert_fusion.1), channel_id=1, source_target_pairs={{0,8},{8,16},{16,24},{24,32},{32,40},{40,48},{48,56},{56,64},{64,7... | collective-permute-start | bytes 6291464 | tf_op jit(solution)/shard_map/ppermute | solution.py:10
  155.7 38.5 %collective-permute-start.1 = (bf16[128,8192]{1,0:T(8,128)(2,1)S(1)}, bf16[128,8192]{1,0:T(8,128)(2,1)S(1)}, u32[]{:S(2)}, u32[]{:S(2)}) collective-permute-start(bf16[128,8192]{1,0:T(8,128)(2,1)S(1)} %convolution_convert_fusion), channel_id=1, source_target_pairs={{8,0},{16,8},{24,16},{32,24},{40,32},{48,40},{56,48},{64,56},{72,6... | collective-permute-start | bytes 6291464 | tf_op jit(solution)/shard_map/ppermute | solution.py:10
Sparse Core Ops, SparseCore 0:
  10.3 137.3 all-gather.1
  196.6 45.5 reduce-scatter.1
where the time goes:
time: 252 us; the launch traced here: 251 us
  waiting for transfers between devices  218 us (87%)
  between operations  14.2 us (6%)
  matrix products  7.52 us (3%)
  other arithmetic  5.05 us (2%)
  starting transfers between devices  4.01 us (2%)
  local copies, waits for them, and re-layouts  2.55 us (1%)
    all_gather x1, waiting for transfers between devices, local(): piece = lax.all_gather(right_env, 'sector', axis=1, tiled=True)  134 us
    reduce_scatter x1, waiting for transfers between devices, local(): lax.psum_scatter(partial_sum.astype(jnp.bfloat16), 'term', scatter_dimens...  45.1 us
    ppermute x2, waiting for transfers between devices, shifted(): lax.ppermute(value, axis, [(source, source + steps) for source in range(i...  37.2 us
  transfers between devices with their start and end apart: 4, of which 4 were waited for; matrix products, arithmetic and copies ran while one was open for 3% of the time, Pallas kernels for 0%

commit v1 on v0

v1 whole, which is shorter than its diff:
```python
import functools

import jax
import jax.numpy as jnp
from jax import lax
from jax.experimental import pallas as pl
from jax.experimental.pallas import tpu as pltpu
from jax.sharding import PartitionSpec as P

MESH = pl.DeviceIdType.MESH
LAG = 2


def kernel(
    nx,
    nz,
    block,
    wave,
    left,
    right,
    left_sizes,
    right_sizes,
    charge_left,
    charge_right,
    shift,
    out,
    rbuf,
    w3,
    l3,
    lcat,
    s1_send,
    s1_recv,
    z_send,
    z_recv,
    x_send,
    x_recv,
    w_send,
    w_recv,
    l_send,
    l_recv,
    g_send,
    g_recv,
):
    ny = nx
    half = nz // 2
    sectors = nx * nz
    terms = 2 * ny
    width = half * block
    s = lax.axis_index("sector")
    t = lax.axis_index("term")
    x = s // nz
    z = lax.rem(s, nz)
    y = t // 2
    c = lax.rem(t, 2)
    own = z // half == c
    own_j = lax.rem(z, half)
    kind = lax.rem(x, 2)
    mirror = jnp.logical_and(jnp.logical_and(own, x == y), c == kind)

    def dev(xx, yy, zz, cc):
        return (xx * nz + zz, yy * 2 + cc)

    x_next = dev(lax.rem(x + 1, nx), y, z, c)
    x_prev = dev(lax.rem(x + nx - 1, nx), y, z, c)
    z_next = dev(x, y, lax.rem(z + 1, nz), c)
    z_prev = dev(x, y, lax.rem(z + nz - 1, nz), c)
    s_next = (lax.rem(s + 1, sectors), t)
    s_prev = (lax.rem(s + sectors - 1, sectors), t)

    column = pl.multiple_of(t * width, 128)
    wave_own = wave.at[:, pl.ds(column, width)]
    left_own = left.at[0, 0]
    w_load = pltpu.make_async_copy(wave_own, w3.at[1], w_recv.at[1])
    l_load = pltpu.make_async_copy(left_own, l3.at[1], l_recv.at[1])
    l_load.start()
    w_load.start()

    barrier = pltpu.get_barrier_semaphore()

    def greet(target):
        pl.semaphore_signal(barrier, inc=1, device_id=target, device_id_type=MESH)

    @pl.when(own)
    def _():
        for yy in range(ny):
            source = dev(y, yy, z, kind)

            @pl.when(jnp.logical_not(jnp.logical_and(mirror, yy == y)))
            def _():
                greet(source)

    for target in (z_next, z_prev, x_next, x_prev, s_next, s_prev):
        greet(target)
    for step in range(1, terms):
        greet((s, lax.rem(t + step, terms)))
    pl.semaphore_wait(barrier, 6 + terms - 1 + nx // 2 - mirror.astype(jnp.int32))

    def remote(src, dst, send_sem, recv_sem, target):
        return pltpu.make_async_remote_copy(
            src_ref=src,
            dst_ref=dst,
            send_sem=send_sem,
            recv_sem=recv_sem,
            device_id=target,
            device_id_type=MESH,
        )

    right_own = right.at[0, 0]
    landing = rbuf.at[own_j, c * ny + y]
    first = [
        remote(right_own, landing, s1_send.at[m], s1_recv.at[y], dev(2 * m + c, x, z, z // half))
        for m in range(nx // 2)
    ]
    for m, copy in enumerate(first):
        itself = jnp.logical_and(mirror, 2 * m + c == x)

        @pl.when(jnp.logical_not(itself))
        def _():
            copy.start()

        @pl.when(itself)
        def _():
            pltpu.make_async_copy(right_own, landing, s1_recv.at[y]).start()

    l_up = remote(left_own, l3.at[0], l_send.at[0], l_recv.at[0], s_next)
    l_down = remote(left_own, l3.at[2], l_send.at[1], l_recv.at[2], s_prev)
    l_up.start()
    l_down.start()
    w_up = remote(wave_own, w3.at[0], w_send.at[0], w_recv.at[0], s_next)
    w_down = remote(wave_own, w3.at[2], w_send.at[1], w_recv.at[2], s_prev)
    w_up.start()
    w_down.start()

    def z_copy(j, sub, side):
        part = rbuf.at[j, pl.ds(kind * ny + sub * (ny // 2), ny // 2)]
        target = z_next if side == 0 else z_prev
        return remote(part, part, z_send.at[j, sub, side], z_recv.at[j, sub], target)

    def x_copy(j, sub):
        part = rbuf.at[j, pl.ds(kind * ny + sub * (ny // 2), ny // 2)]
        target = x_next if sub == 0 else x_prev
        return remote(part, part, x_send.at[j, sub], x_recv.at[j, sub], target)

    def x_wait(j, sub):
        part = rbuf.at[j, pl.ds((1 - kind) * ny + sub * (ny // 2), ny // 2)]
        target = x_next if sub == 0 else x_prev
        remote(part, part, x_send.at[j, sub], x_recv.at[j, sub], target).wait_recv()

    @pl.when(own)
    def _():
        for sub in range(2):
            for yy in range(sub * (ny // 2), (sub + 1) * (ny // 2)):
                block_in = rbuf.at[own_j, kind * ny + yy]
                remote(right_own, block_in, s1_send.at[0], s1_recv.at[yy], s_next).wait_recv()
            z_copy(own_j, sub, 0).start()
            z_copy(own_j, sub, 1).start()
            x_copy(own_j, sub).start()

    l_load.wait()
    l_up.wait_recv()
    l_down.wait_recv()
    place = pl.multiple_of(t * block, 128)
    lanes = pl.ds(place, block)
    lcat[0:block, lanes] = l3[1 - shift[0]]
    lcat[block : block + 16, lanes] = jnp.full((16, block), shift[0], jnp.int32).astype(
        jnp.float32
    ).astype(jnp.bfloat16)
    group = []
    for step in range(1, terms):
        copy = remote(
            lcat.at[:, lanes],
            lcat.at[:, lanes],
            g_send.at[step - 1],
            g_recv.at[t],
            (s, lax.rem(t + step, terms)),
        )
        copy.start()
        group.append(copy)

    def side_flags(k, sub, side):
        origin = lax.rem(z - k + nz if side == 0 else z + k, nz)
        active = origin // half == c
        j = lax.rem(origin, half)
        if sub == side:
            return j, active, jnp.logical_and(active, k < half)
        return (
            j,
            jnp.logical_and(active, k < half),
            jnp.logical_and(active, k < half - 1),
        )

    def move(k):
        for sub in range(2):
            for side in range(2):
                j, has, forward = side_flags(k, sub, side)

                @pl.when(has)
                def _():
                    z_copy(j, sub, side).wait_recv()

                    @pl.when(forward)
                    def _():
                        z_copy(j, sub, side).start()

                    x_copy(j, sub).start()

    def ready():
        w_load.wait()
        w_up.wait_recv()
        w_down.wait_recv()
        for step in range(1, terms):
            peer = lax.rem(t + step, terms)
            part = lcat.at[:, pl.ds(pl.multiple_of(peer * block, 128), block)]
            remote(part, part, g_send.at[0], g_recv.at[peer], s_next).wait_recv()

    row = lax.broadcasted_iota(jnp.int32, (block, block), 0)
    col = lax.broadcasted_iota(jnp.int32, (block, block), 1)

    def compute(j):
        for sub in range(2):
            x_wait(j, sub)
        b = y * nz + c * half + j
        at = pl.ds(pl.multiple_of(j * block, 128), block)
        masked = []
        for d in range(3):
            a = s + d - 1
            inside = jnp.logical_and(a >= 0, a < sectors)
            a = jnp.clip(a, 0, sectors - 1)
            pair = jnp.abs(charge_left[a] - charge_right[b]) <= 1
            rows = jnp.where(inside, left_sizes[a], 0)
            cols = jnp.where(pair, right_sizes[b], 0)
            keep = jnp.logical_and(row < rows, col < cols)
            if d == 1:
                keep_own = keep
            part = w3[d, :, at].astype(jnp.float32)
            masked.append(jnp.where(keep, part, 0.0).astype(jnp.bfloat16))
        inner = []
        for term in range(terms):
            slot = (term % 2) * ny + term // 2
            d = lcat[block : block + 16, term * block : (term + 1) * block].astype(jnp.float32)
            rise = (d * (d + 1.0) * 0.5).astype(jnp.bfloat16)
            fall = (d * (d - 1.0) * 0.5).astype(jnp.bfloat16)
            stay = (1.0 - d * d).astype(jnp.bfloat16)
            rise, fall, stay = (
                jnp.concatenate([m] * (block // 16), axis=0) for m in (rise, fall, stay)
            )
            chosen = masked[1] * stay + masked[0] * rise + masked[2] * fall
            inner.append(
                lax.dot_general(
                    chosen,
                    rbuf[j, slot],
                    (((1,), (1,)), ((), ())),
                    preferred_element_type=jnp.float32,
                ).astype(jnp.bfloat16)
            )
        stacked = jnp.concatenate(inner, axis=0)
        total = jnp.dot(lcat[0:block, :], stacked, preferred_element_type=jnp.float32)
        out[:, at] = jnp.where(keep_own, total, 0.0).astype(jnp.bfloat16)

    @pl.loop(1, half + LAG + 1)
    def _(k):
        @pl.when(k <= half)
        def _():
            move(k)

        @pl.when(k == LAG)
        def _():
            ready()

        @pl.loop(0, 2)
        def _(side):
            kk = k - LAG
            origin = lax.rem(z + nz + jnp.where(side == 0, -kk, kk), nz)
            once = jnp.logical_or(side == 0, jnp.logical_and(kk > 0, kk < half))

            @pl.when(
                jnp.logical_and(jnp.logical_and(kk >= 0, once), origin // half == c)
            )
            def _():
                compute(lax.rem(origin, half))

    for m, copy in enumerate(first):

        @pl.when(jnp.logical_not(jnp.logical_and(mirror, 2 * m + c == x)))
        def _():
            copy.wait_send()

    for copy in (l_up, l_down, w_up, w_down, *group):
        copy.wait_send()

    @pl.when(own)
    def _():
        for sub in range(2):
            z_copy(own_j, sub, 0).wait_send()
            z_copy(own_j, sub, 1).wait_send()

    @pl.loop(1, half)
    def _(k):
        for sub in range(2):
            for side in range(2):
                j, _, forward = side_flags(k, sub, side)

                @pl.when(forward)
                def _():
                    z_copy(j, sub, side).wait_send()

    @pl.loop(0, half)
    def _(j):
        for sub in range(2):
            x_copy(j, sub).wait_send()


def local(nx, nz, wave, left, right, left_sizes, right_sizes, charge_left, charge_right, shift):
    block = left.shape[2]
    half = nz // 2
    terms = 2 * nx
    width = half * block
    hbm = pl.BlockSpec(memory_space=pl.ANY)
    smem = pl.BlockSpec(memory_space=pltpu.SMEM)
    dma = pltpu.SemaphoreType.DMA
    return pl.pallas_call(
        functools.partial(kernel, nx, nz, block),
        out_shape=jax.ShapeDtypeStruct((block, width), jnp.bfloat16),
        in_specs=[hbm] * 3 + [smem] * 5,
        out_specs=pl.BlockSpec(memory_space=pltpu.VMEM),
        scratch_shapes=[
            pltpu.VMEM((half, terms, block, block), jnp.bfloat16),
            pltpu.VMEM((3, block, width), jnp.bfloat16),
            pltpu.VMEM((3, block, block), jnp.bfloat16),
            pltpu.VMEM((block + 16, terms * block), jnp.bfloat16),
            dma((nx // 2,)),
            dma((nx,)),
            dma((half, 2, 2)),
            dma((half, 2)),
            dma((half, 2)),
            dma((half, 2)),
            dma((2,)),
            dma((3,)),
            dma((2,)),
            dma((3,)),
            dma((terms - 1,)),
            dma((terms,)),
        ],
        compiler_params=pltpu.CompilerParams(
            collective_id=0, has_side_effects=True, vmem_limit_bytes=32 << 20
        ),
        cost_estimate=pl.CostEstimate(
            flops=4 * terms * half * block**3, bytes_accessed=1 << 20, transcendentals=0
        ),
    )(wave, left, right, left_sizes, right_sizes, charge_left, charge_right, shift)


def solution(mesh):
    sectors, terms = mesh.shape["sector"], mesh.shape["term"]
    nx = terms // 2
    placed = (
        P("sector", None),
        P("term", "sector", None, None),
        P("term", "sector", None, None),
        P(),
        P(),
        P(),
        P(),
        P("term"),
    )
    return jax.shard_map(
        functools.partial(local, nx, sectors // nx),
        mesh=mesh,
        in_specs=placed,
        out_specs=P("sector", "term"),
        check_vma=False,
    )
```

time: 252 us -> 61.2 us (0.24)
  the two profiles are of different devices: /device:TPU:1 before, /device:TPU:2 now
where the time goes in v1:
time: 61.2 us; the launch traced here: 60.9 us
  Pallas kernels  53.8 us (88%)
  local copies, waits for them, and re-layouts  6.42 us (10%)
  between operations  0.67 us (1%)
    pallas_call x1, Pallas kernels, local(): pl.pallas_call(functools.partial(kernel, nx, nz, block), out_shape=jax.Sh...  53.8 us
    unnamed x15, local copies, waits for them, and re-layouts  6.42 us

profile of v1, /device:TPU:2, one launch (start us, length us, event | category | flops | bytes accessed | tf_op | source)
XLA Modules:
  0.0 60.9 jit_solution(13644155978411736361)
XLA Ops:
  0.7 0.0 copy-start
  0.7 1.6 %copy-done = bf16[128,8192]{1,0:T(8,128)(2,1)S(1)} copy-done((bf16[128,8192]{1,0:T(8,128)(2,1)S(1)}, bf16[128,8192]{1,0:T(8,128)(2,1)}, u32[]{:S(2)}) %copy-start) | copy-done | bytes 2097176
  2.2 0.0 copy-start.1
  2.2 0.8 %copy-done.1 = bf16[1,1,128,128]{3,2,1,0:T(8,128)(2,1)S(1)} copy-done((bf16[1,1,128,128]{3,2,1,0:T(8,128)(2,1)S(1)}, bf16[1,1,128,128]{3,2,1,0:T(8,128)(2,1)}, u32[]{:S(2)}) %copy-start.1) | copy-done | bytes 32792
  3.0 0.0 copy-start.2
  3.0 0.8 %copy-done.2 = bf16[1,1,128,128]{3,2,1,0:T(8,128)(2,1)S(1)} copy-done((bf16[1,1,128,128]{3,2,1,0:T(8,128)(2,1)S(1)}, bf16[1,1,128,128]{3,2,1,0:T(8,128)(2,1)}, u32[]{:S(2)}) %copy-start.2) | copy-done | bytes 32792
  3.8 0.0 copy-start.3
  3.8 0.7 %copy-done.3 = s32[64]{0:T(128)S(1)} copy-done((s32[64]{0:T(128)S(1)}, s32[64]{0:T(128)}, u32[]{:S(2)}) %copy-start.3) | copy-done | bytes 280
  4.4 0.0 copy-start.4
  4.4 0.7 %copy-done.4 = s32[64]{0:T(128)S(1)} copy-done((s32[64]{0:T(128)S(1)}, s32[64]{0:T(128)}, u32[]{:S(2)}) %copy-start.4) | copy-done | bytes 280
  5.1 0.0 copy-start.5
  5.1 0.7 %copy-done.5 = s32[64]{0:T(128)S(1)} copy-done((s32[64]{0:T(128)S(1)}, s32[64]{0:T(128)}, u32[]{:S(2)}) %copy-start.5) | copy-done | bytes 280
  5.7 0.0 copy-start.6
  5.7 0.7 %copy-done.6 = s32[64]{0:T(128)S(1)} copy-done((s32[64]{0:T(128)S(1)}, s32[64]{0:T(128)}, u32[]{:S(2)}) %copy-start.6) | copy-done | bytes 280
  6.4 53.8 %shard_map.82 = bf16[128,1024]{1,0:T(8,128)(2,1)S(1)} custom-call(bf16[128,8192]{1,0:T(8,128)(2,1)S(1)} %copy-done, bf16[1,1,128,128]{3,2,1,0:T(8,128)(2,1)S(1)} %copy-done.1, bf16[1,1,128,128]{3,2,1,0:T(8,128)(2,1)S(1)} %copy-done.2, s32[64]{0:T(128)S(1)} %copy-done.3, s32[64]{0:T(128)S(1)} %copy-done.4, s32[64]{0:T(128)S(1)} %copy-done.5, ...), custom_call_target="tpu_custom_call" | custom-call | flops 536870912 | bytes 1048576 | tf_op jit(solution)/shard_map/pallas_call | solution.py:321
  60.2 0.7 %copy.11 = bf16[128,1024]{1,0:T(8,128)(2,1)} copy(bf16[128,1024]{1,0:T(8,128)(2,1)S(1)} %shard_map.82) | data formatting | bytes 524288
Async XLA Ops:
  0.7 1.6 %copy-start = (bf16[128,8192]{1,0:T(8,128)(2,1)S(1)}, bf16[128,8192]{1,0:T(8,128)(2,1)}, u32[]{:S(2)}) copy-start(bf16[128,8192]{1,0:T(8,128)(2,1)} %wave.1) | copy-start | bytes 6291460
  2.2 0.8 %copy-start.1 = (bf16[1,1,128,128]{3,2,1,0:T(8,128)(2,1)S(1)}, bf16[1,1,128,128]{3,2,1,0:T(8,128)(2,1)}, u32[]{:S(2)}) copy-start(bf16[1,1,128,128]{3,2,1,0:T(8,128)(2,1)} %left.1) | copy-start | bytes 98308
  3.0 0.8 %copy-start.2 = (bf16[1,1,128,128]{3,2,1,0:T(8,128)(2,1)S(1)}, bf16[1,1,128,128]{3,2,1,0:T(8,128)(2,1)}, u32[]{:S(2)}) copy-start(bf16[1,1,128,128]{3,2,1,0:T(8,128)(2,1)} %right.1) | copy-start | bytes 98308
  3.8 0.7 %copy-start.3 = (s32[64]{0:T(128)S(1)}, s32[64]{0:T(128)}, u32[]{:S(2)}) copy-start(s32[64]{0:T(128)} %left_sizes.1) | copy-start | bytes 772
  4.4 0.7 %copy-start.4 = (s32[64]{0:T(128)S(1)}, s32[64]{0:T(128)}, u32[]{:S(2)}) copy-start(s32[64]{0:T(128)} %right_sizes.1) | copy-start | bytes 772
  5.1 0.7 %copy-start.5 = (s32[64]{0:T(128)S(1)}, s32[64]{0:T(128)}, u32[]{:S(2)}) copy-start(s32[64]{0:T(128)} %charge_left.1) | copy-start | bytes 772
  5.7 0.7 %copy-start.6 = (s32[64]{0:T(128)S(1)}, s32[64]{0:T(128)}, u32[]{:S(2)}) copy-start(s32[64]{0:T(128)} %charge_right.1) | copy-start | bytes 772

commit v2 on v1

--- a/solution.py
+++ b/solution.py
@@ -8,7 +8,29 @@
 from jax.sharding import PartitionSpec as P
 
 MESH = pl.DeviceIdType.MESH
-LAG = 2
+
+
+def ring_plan(nz):
+    stride = next(k for k in (5, 3) if nz == 3 * k + 1) if nz % 3 == 1 and nz > 4 else 0
+    entries = (0, stride, nz - stride) if stride else (0,)
+    reach = stride // 2 if stride else nz // 2 - 1
+    steps = []
+    for offset in range(nz):
+        if offset == nz // 2:
+            steps.append((reach + 1, offset, "both", (), ()))
+            continue
+        far = min(
+            ((offset - e + nz // 2) % nz - nz // 2 for e in entries), key=lambda far: abs(far)
+        )
+        up = (0, 1) if 0 <= far < reach else ()
+        down = (0, 1) if -reach < far <= 0 else ()
+        if offset == nz // 2 - 1:
+            up = (0,)
+        if offset == nz // 2 + 1:
+            down = (1,)
+        side = "entry" if far == 0 else ("below" if far > 0 else "above")
+        steps.append((abs(far), offset, side, up, down))
+    return entries, sorted(steps)
 
 
 def kernel(
@@ -18,12 +40,18 @@
     wave,
     left,
     right,
+    left_sizes_in,
+    right_sizes_in,
+    charge_left_in,
+    charge_right_in,
+    shift_in,
+    out,
     left_sizes,
     right_sizes,
     charge_left,
     charge_right,
     shift,
-    out,
+    scalar_sem,
     rbuf,
     w3,
     l3,
@@ -52,10 +80,14 @@
     z = lax.rem(s, nz)
     y = t // 2
     c = lax.rem(t, 2)
-    own = z // half == c
-    own_j = lax.rem(z, half)
     kind = lax.rem(x, 2)
-    mirror = jnp.logical_and(jnp.logical_and(own, x == y), c == kind)
+    entries, steps = ring_plan(nz)
+
+    def meets(offset):
+        origin = lax.rem(z - offset + nz, nz)
+        return origin // half == c, lax.rem(origin, half)
+
+    mirror = jnp.logical_and(jnp.logical_and(z // half == c, x == y), c == kind)
 
     def dev(xx, yy, zz, cc):
         return (xx * nz + zz, yy * 2 + cc)
@@ -74,26 +106,40 @@
     l_load = pltpu.make_async_copy(left_own, l3.at[1], l_recv.at[1])
     l_load.start()
     w_load.start()
+    scalars = [
+        pltpu.make_async_copy(source, held, scalar_sem.at[i])
+        for i, (source, held) in enumerate(
+            (
+                (shift_in, shift),
+                (left_sizes_in, left_sizes),
+                (right_sizes_in, right_sizes),
+                (charge_left_in, charge_left),
+                (charge_right_in, charge_right),
+            )
+        )
+    ]
+    for copy in scalars:
+        copy.start()
 
     barrier = pltpu.get_barrier_semaphore()
 
     def greet(target):
         pl.semaphore_signal(barrier, inc=1, device_id=target, device_id_type=MESH)
 
-    @pl.when(own)
-    def _():
+    for offset in entries:
+        active, _ = meets(offset)
         for yy in range(ny):
-            source = dev(y, yy, z, kind)
-
-            @pl.when(jnp.logical_not(jnp.logical_and(mirror, yy == y)))
+            itself = jnp.logical_and(mirror, yy == y) if offset == 0 else False
+
+            @pl.when(jnp.logical_and(active, jnp.logical_not(itself)))
             def _():
-                greet(source)
+                greet(dev(y, yy, lax.rem(z - offset + nz, nz), kind))
 
     for target in (z_next, z_prev, x_next, x_prev, s_next, s_prev):
         greet(target)
     for step in range(1, terms):
         greet((s, lax.rem(t + step, terms)))
-    pl.semaphore_wait(barrier, 6 + terms - 1 + nx // 2 - mirror.astype(jnp.int32))
+    pl.semaphore_wait(barrier, 6 + terms - 1 + len(entries) * (nx // 2) - mirror.astype(jnp.int32))
 
     def remote(src, dst, send_sem, recv_sem, target):
         return pltpu.make_async_remote_copy(
@@ -105,27 +151,33 @@
             device_id_type=MESH,
         )
 
-    right_own = right.at[0, 0]
-    landing = rbuf.at[own_j, c * ny + y]
-    first = [
-        remote(right_own, landing, s1_send.at[m], s1_recv.at[y], dev(2 * m + c, x, z, z // half))
-        for m in range(nx // 2)
-    ]
-    for m, copy in enumerate(first):
-        itself = jnp.logical_and(mirror, 2 * m + c == x)
-
-        @pl.when(jnp.logical_not(itself))
-        def _():
-            copy.start()
-
-        @pl.when(itself)
-        def _():
-            pltpu.make_async_copy(right_own, landing, s1_recv.at[y]).start()
-
     l_up = remote(left_own, l3.at[0], l_send.at[0], l_recv.at[0], s_next)
     l_down = remote(left_own, l3.at[2], l_send.at[1], l_recv.at[2], s_prev)
     l_up.start()
     l_down.start()
+
+    right_own = right.at[0, 0]
+    landing = rbuf.at[lax.rem(z, half), c * ny + y]
+    landed = s1_recv.at[lax.rem(z, half), y]
+    first = []
+    for e, offset in enumerate(entries):
+        for m in range(nx // 2):
+            target = dev(2 * m + c, x, lax.rem(z + offset, nz), z // half)
+            copy = remote(right_own, landing, s1_send.at[e, m], landed, target)
+            itself = jnp.logical_and(mirror, 2 * m + c == x) if offset == 0 else None
+            first.append((copy, itself))
+            if itself is None:
+                copy.start()
+                continue
+
+            @pl.when(jnp.logical_not(itself))
+            def _():
+                copy.start()
+
+            @pl.when(itself)
+            def _():
+                pltpu.make_async_copy(right_own, landing, landed).start()
+
     w_up = remote(wave_own, w3.at[0], w_send.at[0], w_recv.at[0], s_next)
     w_down = remote(wave_own, w3.at[2], w_send.at[1], w_recv.at[2], s_prev)
     w_up.start()
@@ -146,16 +198,7 @@
         target = x_next if sub == 0 else x_prev
         remote(part, part, x_send.at[j, sub], x_recv.at[j, sub], target).wait_recv()
 
-    @pl.when(own)
-    def _():
-        for sub in range(2):
-            for yy in range(sub * (ny // 2), (sub + 1) * (ny // 2)):
-                block_in = rbuf.at[own_j, kind * ny + yy]
-                remote(right_own, block_in, s1_send.at[0], s1_recv.at[yy], s_next).wait_recv()
-            z_copy(own_j, sub, 0).start()
-            z_copy(own_j, sub, 1).start()
-            x_copy(own_j, sub).start()
-
+    scalars[0].wait()
     l_load.wait()
     l_up.wait_recv()
     l_down.wait_recv()
@@ -177,34 +220,30 @@
         copy.start()
         group.append(copy)
 
-    def side_flags(k, sub, side):
-        origin = lax.rem(z - k + nz if side == 0 else z + k, nz)
-        active = origin // half == c
-        j = lax.rem(origin, half)
-        if sub == side:
-            return j, active, jnp.logical_and(active, k < half)
-        return (
-            j,
-            jnp.logical_and(active, k < half),
-            jnp.logical_and(active, k < half - 1),
-        )
-
-    def move(k):
-        for sub in range(2):
-            for side in range(2):
-                j, has, forward = side_flags(k, sub, side)
-
-                @pl.when(has)
-                def _():
-                    z_copy(j, sub, side).wait_recv()
-
-                    @pl.when(forward)
-                    def _():
-                        z_copy(j, sub, side).start()
-
-                    x_copy(j, sub).start()
+    def move(step):
+        _, offset, side, up, down = step
+        active, j = meets(offset)
+
+        @pl.when(active)
+        def _():
+            for sub in range(2):
+                if side == "entry":
+                    for yy in range(sub * (ny // 2), (sub + 1) * (ny // 2)):
+                        part = rbuf.at[j, kind * ny + yy]
+                        remote(
+                            right_own, part, s1_send.at[0, 0], s1_recv.at[j, yy], s_next
+                        ).wait_recv()
+                else:
+                    z_copy(j, sub, 0).wait_recv()
+                if sub in up:
+                    z_copy(j, sub, 0).start()
+                if sub in down:
+                    z_copy(j, sub, 1).start()
+                x_copy(j, sub).start()
 
     def ready():
+        for copy in scalars[1:]:
+            copy.wait()
         w_load.wait()
         w_up.wait_recv()
         w_down.wait_recv()
@@ -257,52 +296,48 @@
         total = jnp.dot(lcat[0:block, :], stacked, preferred_element_type=jnp.float32)
         out[:, at] = jnp.where(keep_own, total, 0.0).astype(jnp.bfloat16)
 
-    @pl.loop(1, half + LAG + 1)
-    def _(k):
-        @pl.when(k <= half)
+    for step in steps[:-1]:
+        move(step)
+    ready()
+
+    @pl.loop(0, nz)
+    def _(n):
+        @pl.when(n == len(entries))
         def _():
-            move(k)
-
-        @pl.when(k == LAG)
+            move(steps[-1])
+
+        offset = functools.reduce(
+            lambda found, i: jnp.where(n == i, steps[i][1], found), range(1, nz), steps[0][1]
+        )
+        active, j = meets(offset)
+
+        @pl.when(active)
         def _():
-            ready()
-
-        @pl.loop(0, 2)
-        def _(side):
-            kk = k - LAG
-            origin = lax.rem(z + nz + jnp.where(side == 0, -kk, kk), nz)
-            once = jnp.logical_or(side == 0, jnp.logical_and(kk > 0, kk < half))
-
-            @pl.when(
-                jnp.logical_and(jnp.logical_and(kk >= 0, once), origin // half == c)
-            )
-            def _():
-                compute(lax.rem(origin, half))
-
-    for m, copy in enumerate(first):
-
-        @pl.when(jnp.logical_not(jnp.logical_and(mirror, 2 * m + c == x)))
+            compute(j)
+
+    for copy, itself in first:
+        if itself is None:
+            copy.wait_send()
+            continue
+
+        @pl.when(jnp.logical_not(itself))
         def _():
             copy.wait_send()
 
     for copy in (l_up, l_down, w_up, w_down, *group):
         copy.wait_send()
 
-    @pl.when(own)
-    def _():
-        for sub in range(2):
-            z_copy(own_j, sub, 0).wait_send()
-            z_copy(own_j, sub, 1).wait_send()
-
-    @pl.loop(1, half)
-    def _(k):
-        for sub in range(2):
-            for side in range(2):
-                j, _, forward = side_flags(k, sub, side)
-
-                @pl.when(forward)
-                def _():
-                    z_copy(j, sub, side).wait_send()
+    for _, offset, _, up, down in steps:
+        active, j = meets(offset)
+        if not up + down:
+            continue
+
+        @pl.when(active)
+        def _():
+            for sub in up:
+                z_copy(j, sub, 0).wait_send()
+            for sub in down:
+                z_copy(j, sub, 1).wait_send()
 
     @pl.loop(0, half)
     def _(j):
@@ -316,20 +351,27 @@
     terms = 2 * nx
     width = half * block
     hbm = pl.BlockSpec(memory_space=pl.ANY)
-    smem = pl.BlockSpec(memory_space=pltpu.SMEM)
+    sectors = nx * nz
+    entries, _ = ring_plan(nz)
     dma = pltpu.SemaphoreType.DMA
     return pl.pallas_call(
         functools.partial(kernel, nx, nz, block),
         out_shape=jax.ShapeDtypeStruct((block, width), jnp.bfloat16),
-        in_specs=[hbm] * 3 + [smem] * 5,
+        in_specs=[hbm] * 8,
         out_specs=pl.BlockSpec(memory_space=pltpu.VMEM),
         scratch_shapes=[
+            pltpu.SMEM((sectors,), jnp.int32),
+            pltpu.SMEM((sectors,), jnp.int32),
+            pltpu.SMEM((sectors,), jnp.int32),
+            pltpu.SMEM((sectors,), jnp.int32),
+            pltpu.SMEM((1,), jnp.int32),
+            dma((5,)),
             pltpu.VMEM((half, terms, block, block), jnp.bfloat16),
             pltpu.VMEM((3, block, width), jnp.bfloat16),
             pltpu.VMEM((3, block, block), jnp.bfloat16),
             pltpu.VMEM((block + 16, terms * block), jnp.bfloat16),
-            dma((nx // 2,)),
-            dma((nx,)),
+            dma((len(entries), nx // 2)),
+            dma((half, nx)),
             dma((half, 2, 2)),
             dma((half, 2)),
             dma((half, 2)),
@@ -342,7 +384,7 @@
             dma((terms,)),
         ],
         compiler_params=pltpu.CompilerParams(
-            collective_id=0, has_side_effects=True, vmem_limit_bytes=32 << 20
+            collective_id=0, has_side_effects=True, vmem_limit_bytes=60 << 20
         ),
         cost_estimate=pl.CostEstimate(
             flops=4 * terms * half * block**3, bytes_accessed=1 << 20, transcendentals=0

time: 61.2 us -> 53.1 us (0.87)
  the two profiles are of different devices: /device:TPU:2 before, /device:TPU:1 now
where the time goes in v2:
time: 53.1 us; the launch traced here: 53 us
  Pallas kernels  50.7 us (95%)
  local copies, waits for them, and re-layouts  1.67 us (3%)
  between operations  0.66 us (1%)
    pallas_call x1, Pallas kernels, local(): pl.pallas_call(functools.partial(kernel, nx, nz, block), out_shape=jax.Sh...  50.7 us
    unnamed x1, local copies, waits for them, and re-layouts  1.67 us

profile of v2, /device:TPU:1, one launch (start us, length us, event | category | flops | bytes accessed | tf_op | source)
XLA Modules:
  0.0 53.0 jit_solution(18271702577518080839)
XLA Ops:
  0.7 50.7 %shard_map.82 = bf16[128,1024]{1,0:T(8,128)(2,1)} custom-call(bf16[128,8192]{1,0:T(8,128)(2,1)} %wave.1, bf16[1,1,128,128]{3,2,1,0:T(8,128)(2,1)} %left.1, bf16[1,1,128,128]{3,2,1,0:T(8,128)(2,1)} %right.1, s32[64]{0:T(128)} %left_sizes_in.1, s32[64]{0:T(128)} %right_sizes_in.1, s32[64]{0:T(128)} %charge_left_in.1, s32[64]{0:T(128)} %charge_right_in.1, ...), custom_call_target="tpu_custom_call" | custom-call | flops 536870912 | bytes 1048576 | tf_op jit(solution)/shard_map/pallas_call | solution.py:357
  51.3 1.7 %copy.11 = bf16[128,1024]{1,0:T(8,128)(2,1)} copy(bf16[128,1024]{1,0:T(8,128)(2,1)} %shard_map.82) | data formatting | bytes 524288

commit v3 on v0

v3 whole, which is shorter than its diff:
```python
import functools

import jax
import jax.numpy as jnp
from jax import lax
from jax.experimental import pallas as pl
from jax.experimental.pallas import tpu as pltpu
from jax.sharding import PartitionSpec as P

MESH = pl.DeviceIdType.MESH
PIECES = 4


def ring_plan(nz):
    entries = (0, 5, 11) if nz == 16 else (0, 3, 7) if nz == 10 else (0,)
    middle = nz // 2
    near = max(e for e in entries if e < middle)

    def comes(offset):
        if offset == middle:
            return 1.5, 0
        below = min((offset - e) % nz for e in entries)
        above = min((e - offset) % nz for e in entries)
        return (0, 0) if below == 0 else (below, 1) if below < above else (above, -1)

    depths = []
    for depth in sorted({comes(offset)[0] for offset in range(nz)}):
        have = [offset for offset in range(nz) if comes(offset)[0] == depth]
        up = [offset for offset in have if comes((offset + 1) % nz)[1] == 1]
        down = [offset for offset in have if comes((offset - 1) % nz)[1] == -1]
        jump_up = [offset for offset in have if offset == near]
        jump_down = [offset for offset in have if offset == (nz - near) % nz]
        depths.append((have, up, down, (jump_up, jump_down)))
    return entries, middle - near, depths


def one_of(value, choices):
    return functools.reduce(jnp.logical_or, [value == choice for choice in choices])


def kernel(
    nx,
    nz,
    block,
    wave,
    left,
    right,
    left_sizes_in,
    right_sizes_in,
    charge_left_in,
    charge_right_in,
    shift_in,
    out,
    left_sizes,
    right_sizes,
    charge_left,
    charge_right,
    shift,
    scalar_sem,
    rbuf,
    w3,
    l3,
    lbuf,
    mw,
    inner,
    obuf,
    s1_send,
    s1_recv,
    z_send,
    z_recv,
    jump_send,
    w_send,
    w_recv,
    l_send,
    l_recv,
    lx_send,
    lx_recv,
    ly_send,
    ly_recv,
    sib_send,
    sib_recv,
    o_send,
    o_recv,
):
    ny = nx
    half = nz // 2
    share = half // nx
    sectors = nx * nz
    terms = 2 * ny
    width = half * block
    part_width = share * block
    s = lax.axis_index("sector")
    t = lax.axis_index("term")
    x = s // nz
    z = lax.rem(s, nz)
    y = t // 2
    c = lax.rem(t, 2)
    entries, jump, depths = ring_plan(nz)

    def dev(xx, yy, zz, cc):
        return (xx * nz + zz, yy * 2 + cc)

    def along(value, step, size):
        return lax.rem(value + step + size, size)

    origins = [c * half + x * share + q for q in range(share)]
    roles = [lax.rem(z - origin + nz, nz) for origin in origins]
    above, below = along(z, 1, nz), along(z, -1, nz)
    z_sides = (dev(x, y, above, c), dev(x, y, below, c))
    z_jumps = (dev(x, y, along(z, jump, nz), c), dev(x, y, along(z, -jump, nz), c))
    sibling = (s, t + 1 - 2 * c)
    s_next, s_prev = lax.rem(s + 1, sectors), lax.rem(s + sectors - 1, sectors)

    ring_x, ring_c = lax.rem(z, half) // share, z // half
    mirror = jnp.logical_and(jnp.logical_and(ring_x == x, x == y), ring_c == c)

    def columns(xx):
        start = pl.multiple_of(t * width + xx * part_width, 128)
        return wave.at[:, pl.ds(start, part_width)]

    left_own = left.at[0, 0]
    w_load = pltpu.make_async_copy(columns(x), w3.at[1, x], w_recv.at[1, x])
    l_load = pltpu.make_async_copy(left_own, l3.at[1], l_recv.at[1])
    l_load.start()
    w_load.start()
    scalars = [
        pltpu.make_async_copy(source, held, scalar_sem.at[i])
        for i, (source, held) in enumerate(
            (
                (shift_in, shift),
                (left_sizes_in, left_sizes),
                (right_sizes_in, right_sizes),
                (charge_left_in, charge_left),
                (charge_right_in, charge_right),
            )
        )
    ]
    for copy in scalars:
        copy.start()

    barrier = pltpu.get_barrier_semaphore()

    def greet(target):
        pl.semaphore_signal(barrier, inc=1, device_id=target, device_id_type=MESH)

    for q in range(share):

        @pl.when(one_of(roles[q], entries))
        def _():
            for yy in range(ny):
                for cc in range(2):
                    itself = jnp.logical_and(
                        jnp.logical_and(x == y, z == origins[q]),
                        jnp.logical_and(yy == y, cc == c),
                    )

                    @pl.when(jnp.logical_not(itself))
                    def _():
                        greet(dev(y, yy, origins[q], cc))

    for xx in range(nx):
        greet(dev(xx, y, above, c))
        greet(dev(xx, y, below, c))
    for target in (*z_jumps, sibling):
        greet(target)
    for k in range(1, nx):
        greet(dev(along(x, k, nx), y, z, c))
        greet(dev(x, along(y, k, ny), z, c))
    partners = 2 * nx + 3 + 2 * (nx - 1)
    pl.semaphore_wait(barrier, partners + len(entries) - mirror.astype(jnp.int32))

    def remote(src, dst, send_sem, recv_sem, target):
        return pltpu.make_async_remote_copy(
            src_ref=src,
            dst_ref=dst,
            send_sem=send_sem,
            recv_sem=recv_sem,
            device_id=target,
            device_id_type=MESH,
        )

    l_up = remote(left_own, l3.at[0], l_send.at[0], l_recv.at[0], (s_next, t))
    l_down = remote(left_own, l3.at[2], l_send.at[1], l_recv.at[2], (s_prev, t))
    l_up.start()
    l_down.start()

    right_own = right.at[0, 0]
    own_q = lax.rem(z, share)
    landing, landed = rbuf.at[own_q, t], s1_recv.at[own_q, t]
    first = [
        remote(right_own, landing, s1_send.at[e], landed, dev(ring_x, x, along(z, off, nz), ring_c))
        for e, off in enumerate(entries)
    ]
    for copy in first[1:]:
        copy.start()

    @pl.when(mirror)
    def _():
        pltpu.make_async_copy(right_own, landing, landed).start()

    @pl.when(jnp.logical_not(mirror))
    def _():
        first[0].start()

    waves = []
    for d, row_to in ((0, s_next), (2, s_prev)):
        for xx in range(nx):
            target = dev(xx, y, lax.rem(row_to, nz), c)
            dst = w3.at[d, row_to // nz]
            waves.append(
                remote(columns(xx), dst, w_send.at[d, xx], w_recv.at[d, row_to // nz], target)
            )
    for k in range(1, nx):
        xx = along(x, k, nx)
        waves.append(
            remote(columns(xx), w3.at[1, x], w_send.at[1, k], w_recv.at[1, x], dev(xx, y, z, c))
        )

    scalars[0].wait()
    l_load.wait()
    l_up.wait_recv()
    l_down.wait_recv()
    lbuf[c, y, x, 0:block, :] = l3[1 - shift[0]]
    lbuf[c, y, x, block : block + 16, :] = (
        jnp.full((16, block), shift[0], jnp.int32).astype(jnp.float32).astype(jnp.bfloat16)
    )

    def along_x(k, of):
        part = lbuf.at[c, y, of]
        target = dev(along(x, k, nx), y, z, c)
        return remote(part, part, lx_send.at[k - 1], lx_recv.at[k - 1], target)

    def along_y(k, of):
        part = lbuf.at[c, of]
        target = dev(x, along(y, k, ny), z, c)
        return remote(part, part, ly_send.at[k - 1], ly_recv.at[k - 1], target)

    def to_sibling(k, of, core):
        part = lbuf.at[core, of]
        return remote(part, part, sib_send.at[k], sib_recv.at[k], sibling)

    for k in range(1, nx):
        along_x(k, x).start()

    blocks = terms // PIECES

    def z_part(q, sub):
        return rbuf.at[q, pl.ds(sub * blocks, blocks)]

    def z_copy(q, sub, side):
        part = z_part(q, sub)
        return remote(part, part, z_send.at[q, sub, side], z_recv.at[q, sub], z_sides[side])

    def z_jump(q, sub):
        part = z_part(q, sub)
        return remote(part, part, jump_send.at[q, sub], z_recv.at[q, sub], z_jumps[2 * sub // PIECES])

    def when_role(q, offsets, act):
        if offsets:
            pl.when(one_of(roles[q], offsets))(act)

    for have, up, down, jumps in depths:
        for q in range(share):

            def pass_on(q=q, have=have, up=up, down=down, jumps=jumps):
                for sub in range(PIECES):
                    if have[0] in entries:
                        for k in range(sub * blocks, (sub + 1) * blocks):
                            copy = remote(
                                right_own, rbuf.at[q, k], s1_send.at[0], s1_recv.at[q, k], sibling
                            )
                            copy.wait_recv()
                    else:
                        z_copy(q, sub, 0).wait_recv()
                    when_role(q, jumps[2 * sub // PIECES], lambda: z_jump(q, sub).start())
                    when_role(q, up, lambda: z_copy(q, sub, 0).start())
                    when_role(q, down, lambda: z_copy(q, sub, 1).start())

            when_role(q, have, pass_on)
        if have[0] in entries:
            for k in range(1, nx):
                along_x(k, along(x, -k, nx)).wait_recv()
            for k in range(1, ny):
                along_y(k, y).start()
            to_sibling(0, y, c).start()
            for copy in waves:
                copy.start()

    for k in range(1, ny):
        of = along(y, -k, ny)
        along_y(k, of).wait_recv()
        to_sibling(k, of, c).start()
    for copy in scalars[1:]:
        copy.wait()
    w_load.wait()
    for d in range(3):
        for k in range(nx):
            of = along(x, k, nx)
            if d == 1 and k == 0:
                continue
            part = w3.at[d, of]
            remote(part, part, w_send.at[d, 0], w_recv.at[d, of], sibling).wait_recv()
    for k in range(ny):
        to_sibling(k, along(y, -k, ny), 1 - c).wait_recv()

    row = lax.broadcasted_iota(jnp.int32, (block, block), 0)
    col = lax.broadcasted_iota(jnp.int32, (block, block), 1)

    def allowed(a, b):
        inside = jnp.logical_and(a >= 0, a < sectors)
        a = jnp.clip(a, 0, sectors - 1)
        pair = jnp.abs(charge_left[a] - charge_right[b]) <= 1
        rows = jnp.where(inside, left_sizes[a], 0)
        cols = jnp.where(pair, right_sizes[b], 0)
        return jnp.logical_and(row < rows, col < cols)

    def ship(q, k, of):
        xx = along(x, k, nx)
        place = pl.multiple_of(of * part_width + q * block, 128)
        dst = out.at[:, pl.ds(place, block)]
        return remote(
            obuf.at[q, xx], dst, o_send.at[q, k - 1], o_recv.at[q, k - 1], dev(xx, y, z, c)
        )

    @pl.loop(0, share)
    def _(q):
        b = y * nz + c * half + x * share + q
        at = pl.ds(pl.multiple_of(q * block, 128), block)
        for xx in range(nx):
            for d in range(3):
                part = w3[d, xx, :, at].astype(jnp.float32)
                keep = allowed(nz * xx + z + d - 1, b)
                mw[d, xx * block : (xx + 1) * block, :] = jnp.where(keep, part, 0.0).astype(
                    jnp.bfloat16
                )
        for term in range(terms):
            d = lbuf[term % 2, term // 2, 0, block : block + 16, :].astype(jnp.float32)
            rise = (d * (d + 1.0) * 0.5).astype(jnp.bfloat16)
            fall = (d * (d - 1.0) * 0.5).astype(jnp.bfloat16)
            stay = (1.0 - d * d).astype(jnp.bfloat16)
            rise, fall, stay = (
                jnp.concatenate([m] * (nx * block // 16), axis=0) for m in (rise, fall, stay)
            )
            chosen = mw[1] * stay + mw[0] * rise + mw[2] * fall
            product = lax.dot_general(
                chosen, rbuf[q, term], (((1,), (1,)), ((), ())), preferred_element_type=jnp.float32
            ).astype(jnp.bfloat16)
            for xx in range(nx):
                inner[xx, term * block : (term + 1) * block, :] = product[
                    xx * block : (xx + 1) * block
                ]
        for xx in range(nx):
            lefts = jnp.concatenate(
                [lbuf[term % 2, term // 2, xx, 0:block, :] for term in range(terms)], axis=1
            )
            total = jnp.dot(lefts, inner[xx], preferred_element_type=jnp.float32)
            keep = allowed(nz * xx + z, b)
            obuf[q, xx] = jnp.where(keep, total, 0.0).astype(jnp.bfloat16)
        for k in range(1, nx):
            ship(q, k, x).start()
        place = pl.multiple_of(x * part_width + q * block, 128)
        out[:, pl.ds(place, block)] = obuf[q, x]

    for copy in first[1:]:
        copy.wait_send()

    @pl.when(jnp.logical_not(mirror))
    def _():
        first[0].wait_send()

    for copy in (l_up, l_down, *waves):
        copy.wait_send()
    for k in range(1, nx):
        along_x(k, x).wait_send()
        along_y(k, y).wait_send()
    to_sibling(0, y, c).wait_send()
    for k in range(1, ny):
        to_sibling(k, along(y, -k, ny), c).wait_send()
    for _, up, down, jumps in depths:
        for q in range(share):
            for sub in range(PIECES):
                when_role(q, jumps[2 * sub // PIECES], lambda: z_jump(q, sub).wait_send())
                when_role(q, up, lambda: z_copy(q, sub, 0).wait_send())
                when_role(q, down, lambda: z_copy(q, sub, 1).wait_send())
    for q in range(share):
        for k in range(1, nx):
            ship(q, k, x).wait_send()
            ship(q, k, along(x, -k, nx)).wait_recv()


def local(nx, nz, wave, left, right, left_sizes, right_sizes, charge_left, charge_right, shift):
    block = left.shape[2]
    ny = nx
    half = nz // 2
    share = half // nx
    terms = 2 * ny
    sectors = nx * nz
    entries, _, _ = ring_plan(nz)
    hbm = pl.BlockSpec(memory_space=pl.ANY)
    dma = pltpu.SemaphoreType.DMA
    half_float = jnp.bfloat16
    return pl.pallas_call(
        functools.partial(kernel, nx, nz, block),
        out_shape=jax.ShapeDtypeStruct((block, half * block), jnp.bfloat16),
        in_specs=[hbm] * 8,
        out_specs=pl.BlockSpec(memory_space=pltpu.VMEM),
        scratch_shapes=[
            pltpu.SMEM((sectors,), jnp.int32),
            pltpu.SMEM((sectors,), jnp.int32),
            pltpu.SMEM((sectors,), jnp.int32),
            pltpu.SMEM((sectors,), jnp.int32),
            pltpu.SMEM((1,), jnp.int32),
            dma((5,)),
            pltpu.VMEM((share, terms, block, block), half_float),
            pltpu.VMEM((3, nx, block, share * block), half_float),
            pltpu.VMEM((3, block, block), half_float),
            pltpu.VMEM((2, ny, nx, block + 16, block), half_float),
            pltpu.VMEM((3, nx * block, block), half_float),
            pltpu.VMEM((nx, terms * block, block), half_float),
            pltpu.VMEM((share, nx, block, block), half_float),
            dma((len(entries),)),
            dma((share, terms)),
            dma((share, PIECES, 2)),
            dma((share, PIECES)),
            dma((share, PIECES)),
            dma((3, nx)),
            dma((3, nx)),
            dma((2,)),
            dma((3,)),
            dma((nx - 1,)),
            dma((nx - 1,)),
            dma((ny - 1,)),
            dma((ny - 1,)),
            dma((ny,)),
            dma((ny,)),
            dma((share, nx - 1)),
            dma((share, nx - 1)),
        ],
        compiler_params=pltpu.CompilerParams(
            collective_id=0, has_side_effects=True, vmem_limit_bytes=60 << 20
        ),
        cost_estimate=pl.CostEstimate(
            flops=4 * terms * half * block**3, bytes_accessed=1 << 20, transcendentals=0
        ),
    )(wave, left, right, left_sizes, right_sizes, charge_left, charge_right, shift)


def solution(mesh):
    sectors, terms = mesh.shape["sector"], mesh.shape["term"]
    nx = terms // 2
    placed = (
        P("sector", None),
        P("term", "sector", None, None),
        P("term", "sector", None, None),
        P(),
        P(),
        P(),
        P(),
        P("term"),
    )
    return jax.shard_map(
        functools.partial(local, nx, sectors // nx),
        mesh=mesh,
        in_specs=placed,
        out_specs=P("sector", "term"),
        check_vma=False,
    )
```

time: 252 us -> 50.9 us (0.20)
  waiting for transfers between devices: 218 us -> 0 us
  Pallas kernels: 0 us -> 48.4 us
  between operations: 14.2 us -> 0.66 us
  matrix products: 7.52 us -> 0 us
  other arithmetic: 5.05 us -> 0 us
  starting transfers between devices: 4.01 us -> 0 us
    all_gather x1 -> x0, waiting for transfers between devices: 134 us -> none  [local(): piece = lax.all_gather(right_env, 'sector', axis=1, tiled=True)]
    pallas_call x0 -> x1, Pallas kernels: none -> 48.4 us  [local(): pl.pallas_call(functools.partial(kernel, nx, nz, block), out_shape=jax.Sh...]
    reduce_scatter x1 -> x0, waiting for transfers between devices: 45.1 us -> none  [local(): lax.psum_scatter(partial_sum.astype(jnp.bfloat16), 'term', scatter_dimens...]
    ppermute x2 -> x0, waiting for transfers between devices: 37.2 us -> none  [shifted(): lax.ppermute(value, axis, [(source, source + steps) for source in range(i...]
    dot_general x4 -> x0, matrix products: 7.52 us -> none  [the longest x1 3.86 us: local(): jnp.einsum('ibj,tbkj->tibk', columns, piece, preferred_element_type=jnp.f...]
    ppermute x2 -> x0, starting transfers between devices: 3.97 us -> none  [shifted(): lax.ppermute(value, axis, [(source, source + steps) for source in range(i...]
    dynamic_slice x2 -> x0, local copies, waits for them, and re-layouts: 2.55 us -> none  [the longest x1 1.3 us: local(): row_ok = place < left_sizes[own_sector]]
  transfers between devices with their start and end apart: 4 -> 0, of which waited for: 4 -> 0; matrix products, arithmetic and copies ran while one was open for 3% -> 0% of each run, Pallas kernels for 0% -> 0%
where the time goes in v3:
time: 50.9 us; the launch traced here: 50.7 us
  Pallas kernels  48.4 us (95%)
  local copies, waits for them, and re-layouts  1.67 us (3%)
  between operations  0.66 us (1%)
    pallas_call x1, Pallas kernels, local(): pl.pallas_call(functools.partial(kernel, nx, nz, block), out_shape=jax.Sh...  48.4 us
    unnamed x1, local copies, waits for them, and re-layouts  1.67 us

profile of v3, /device:TPU:1, one launch (start us, length us, event | category | flops | bytes accessed | tf_op | source)
XLA Modules:
  0.0 50.7 jit_solution(870369244382179773)
XLA Ops:
  0.7 48.4 %shard_map.82 = bf16[128,1024]{1,0:T(8,128)(2,1)} custom-call(bf16[128,8192]{1,0:T(8,128)(2,1)} %wave.1, bf16[1,1,128,128]{3,2,1,0:T(8,128)(2,1)} %left.1, bf16[1,1,128,128]{3,2,1,0:T(8,128)(2,1)} %right.1, s32[64]{0:T(128)} %left_sizes_in.1, s32[64]{0:T(128)} %right_sizes_in.1, s32[64]{0:T(128)} %charge_left_in.1, s32[64]{0:T(128)} %charge_right_in.1, ...), custom_call_target="tpu_custom_call" | custom-call | flops 536870912 | bytes 1048576 | tf_op jit(solution)/shard_map/pallas_call | solution.py:402
  49.1 1.7 %copy.11 = bf16[128,1024]{1,0:T(8,128)(2,1)} copy(bf16[128,1024]{1,0:T(8,128)(2,1)} %shard_map.82) | data formatting | bytes 524288

commit v4 on v3

--- a/solution.py
+++ b/solution.py
@@ -14,11 +14,11 @@
 def ring_plan(nz):
     entries = (0, 5, 11) if nz == 16 else (0, 3, 7) if nz == 10 else (0,)
     middle = nz // 2
-    near = max(e for e in entries if e < middle)
+    near = middle - 1
 
     def comes(offset):
         if offset == middle:
-            return 1.5, 0
+            return nz, 0
         below = min((offset - e) % nz for e in entries)
         above = min((e - offset) % nz for e in entries)
         return (0, 0) if below == 0 else (below, 1) if below < above else (above, -1)
@@ -241,6 +241,8 @@
 
     for k in range(1, nx):
         along_x(k, x).start()
+    for copy in waves[: 2 * nx]:
+        copy.start()
 
     blocks = terms // PIECES
 
@@ -277,19 +279,20 @@
                     when_role(q, down, lambda: z_copy(q, sub, 1).start())
 
             when_role(q, have, pass_on)
+        if have is depths[min(2, len(depths) - 1)][0]:
+            for k in range(1, ny):
+                of = along(y, -k, ny)
+                along_y(k, of).wait_recv()
+                to_sibling(k, of, c).start()
         if have[0] in entries:
             for k in range(1, nx):
                 along_x(k, along(x, -k, nx)).wait_recv()
             for k in range(1, ny):
                 along_y(k, y).start()
             to_sibling(0, y, c).start()
-            for copy in waves:
+            for copy in waves[2 * nx :]:
                 copy.start()
 
-    for k in range(1, ny):
-        of = along(y, -k, ny)
-        along_y(k, of).wait_recv()
-        to_sibling(k, of, c).start()
     for copy in scalars[1:]:
         copy.wait()
     w_load.wait()

time: 50.9 us -> 50.1 us (0.984)
  Pallas kernels: 48.4 us -> 47.6 us
    pallas_call x1, Pallas kernels: 48.4 us -> 47.6 us  [local(): pl.pallas_call(functools.partial(kernel, nx, nz, block), out_shape=jax.Sh...]
where the time goes in v4:
time: 50.1 us; the launch traced here: 49.9 us
  Pallas kernels  47.6 us (95%)
  local copies, waits for them, and re-layouts  1.67 us (3%)
  between operations  0.66 us (1%)
    pallas_call x1, Pallas kernels, local(): pl.pallas_call(functools.partial(kernel, nx, nz, block), out_shape=jax.Sh...  47.6 us
    unnamed x1, local copies, waits for them, and re-layouts  1.67 us

profile of v4, /device:TPU:1, one launch (start us, length us, event | category | flops | bytes accessed | tf_op | source)
XLA Modules:
  0.0 49.9 jit_solution(6833667674107486324)
XLA Ops:
  0.7 47.6 %shard_map.82 = bf16[128,1024]{1,0:T(8,128)(2,1)} custom-call(bf16[128,8192]{1,0:T(8,128)(2,1)} %wave.1, bf16[1,1,128,128]{3,2,1,0:T(8,128)(2,1)} %left.1, bf16[1,1,128,128]{3,2,1,0:T(8,128)(2,1)} %right.1, s32[64]{0:T(128)} %left_sizes_in.1, s32[64]{0:T(128)} %right_sizes_in.1, s32[64]{0:T(128)} %charge_left_in.1, s32[64]{0:T(128)} %charge_right_in.1, ...), custom_call_target="tpu_custom_call" | custom-call | flops 536870912 | bytes 1048576 | tf_op jit(solution)/shard_map/pallas_call | solution.py:405
  48.3 1.7 %copy.11 = bf16[128,1024]{1,0:T(8,128)(2,1)} copy(bf16[128,1024]{1,0:T(8,128)(2,1)} %shard_map.82) | data formatting | bytes 524288

commit v5 on v4

--- a/solution.py
+++ b/solution.py
@@ -81,6 +81,7 @@
     sib_recv,
     o_send,
     o_recv,
+    own_sem,
 ):
     ny = nx
     half = nz // 2
@@ -279,6 +280,9 @@
                     when_role(q, down, lambda: z_copy(q, sub, 1).start())
 
             when_role(q, have, pass_on)
+        if have is depths[1][0]:
+            for copy in waves[2 * nx :]:
+                copy.start()
         if have is depths[min(2, len(depths) - 1)][0]:
             for k in range(1, ny):
                 of = along(y, -k, ny)
@@ -290,8 +294,6 @@
             for k in range(1, ny):
                 along_y(k, y).start()
             to_sibling(0, y, c).start()
-            for copy in waves[2 * nx :]:
-                copy.start()
 
     for copy in scalars[1:]:
         copy.wait()
@@ -324,6 +326,10 @@
         return remote(
             obuf.at[q, xx], dst, o_send.at[q, k - 1], o_recv.at[q, k - 1], dev(xx, y, z, c)
         )
+
+    def keep_own(q):
+        place = pl.multiple_of(x * part_width + q * block, 128)
+        return pltpu.make_async_copy(obuf.at[q, x], out.at[:, pl.ds(place, block)], own_sem.at[q])
 
     @pl.loop(0, share)
     def _(q):
@@ -361,8 +367,7 @@
             obuf[q, xx] = jnp.where(keep, total, 0.0).astype(jnp.bfloat16)
         for k in range(1, nx):
             ship(q, k, x).start()
-        place = pl.multiple_of(x * part_width + q * block, 128)
-        out[:, pl.ds(place, block)] = obuf[q, x]
+        keep_own(q).start()
 
     for copy in first[1:]:
         copy.wait_send()
@@ -386,6 +391,7 @@
                 when_role(q, up, lambda: z_copy(q, sub, 0).wait_send())
                 when_role(q, down, lambda: z_copy(q, sub, 1).wait_send())
     for q in range(share):
+        keep_own(q).wait()
         for k in range(1, nx):
             ship(q, k, x).wait_send()
             ship(q, k, along(x, -k, nx)).wait_recv()
@@ -406,7 +412,7 @@
         functools.partial(kernel, nx, nz, block),
         out_shape=jax.ShapeDtypeStruct((block, half * block), jnp.bfloat16),
         in_specs=[hbm] * 8,
-        out_specs=pl.BlockSpec(memory_space=pltpu.VMEM),
+        out_specs=pl.BlockSpec(memory_space=pl.ANY),
         scratch_shapes=[
             pltpu.SMEM((sectors,), jnp.int32),
             pltpu.SMEM((sectors,), jnp.int32),
@@ -438,6 +444,7 @@
             dma((ny,)),
             dma((share, nx - 1)),
             dma((share, nx - 1)),
+            dma((share,)),
         ],
         compiler_params=pltpu.CompilerParams(
             collective_id=0, has_side_effects=True, vmem_limit_bytes=60 << 20

time: 50.1 us -> 49.5 us (0.988)
  Pallas kernels: 47.6 us -> 47 us
    pallas_call x1, Pallas kernels: 47.6 us -> 47 us  [local(): pl.pallas_call(functools.partial(kernel, nx, nz, block), out_shape=jax.Sh...]
where the time goes in v5:
time: 49.5 us; the launch traced here: 49.4 us
  Pallas kernels  47 us (95%)
  local copies, waits for them, and re-layouts  1.67 us (3%)
  between operations  0.66 us (1%)
    pallas_call x1, Pallas kernels, local(): pl.pallas_call(functools.partial(kernel, nx, nz, block), out_shape=jax.Sh...  47 us
    unnamed x1, local copies, waits for them, and re-layouts  1.67 us

profile of v5, /device:TPU:1, one launch (start us, length us, event | category | flops | bytes accessed | tf_op | source)
XLA Modules:
  0.0 49.4 jit_solution(13197186638948262674)
XLA Ops:
  0.7 47.0 %shard_map.82 = bf16[128,1024]{1,0:T(8,128)(2,1)} custom-call(bf16[128,8192]{1,0:T(8,128)(2,1)} %wave.1, bf16[1,1,128,128]{3,2,1,0:T(8,128)(2,1)} %left.1, bf16[1,1,128,128]{3,2,1,0:T(8,128)(2,1)} %right.1, s32[64]{0:T(128)} %left_sizes_in.1, s32[64]{0:T(128)} %right_sizes_in.1, s32[64]{0:T(128)} %charge_left_in.1, s32[64]{0:T(128)} %charge_right_in.1, ...), custom_call_target="tpu_custom_call" | custom-call | flops 536870912 | bytes 1048576 | tf_op jit(solution)/shard_map/pallas_call | solution.py:411
  47.7 1.7 %copy.11 = bf16[128,1024]{1,0:T(8,128)(2,1)} copy(bf16[128,1024]{1,0:T(8,128)(2,1)} %shard_map.82) | data formatting | bytes 524288

commit v6 on v5

--- a/solution.py
+++ b/solution.py
@@ -365,7 +365,7 @@
             total = jnp.dot(lefts, inner[xx], preferred_element_type=jnp.float32)
             keep = allowed(nz * xx + z, b)
             obuf[q, xx] = jnp.where(keep, total, 0.0).astype(jnp.bfloat16)
-        for k in range(1, nx):
+        for k in sorted(range(1, nx), key=lambda k: -min(k, nx - k)):
             ship(q, k, x).start()
         keep_own(q).start()
 

time: 49.5 us -> 49.2 us (level)
  no operation moved by 1% of the time
where the time goes in v6:
time: 49.2 us; the launch traced here: 49.1 us
  Pallas kernels  46.8 us (95%)
  local copies, waits for them, and re-layouts  1.67 us (3%)
  between operations  0.66 us (1%)
    pallas_call x1, Pallas kernels, local(): pl.pallas_call(functools.partial(kernel, nx, nz, block), out_shape=jax.Sh...  46.8 us
    unnamed x1, local copies, waits for them, and re-layouts  1.67 us

profile of v6, /device:TPU:1, one launch (start us, length us, event | category | flops | bytes accessed | tf_op | source)
XLA Modules:
  0.0 49.1 jit_solution(12357338446654962390)
XLA Ops:
  0.7 46.8 %shard_map.82 = bf16[128,1024]{1,0:T(8,128)(2,1)} custom-call(bf16[128,8192]{1,0:T(8,128)(2,1)} %wave.1, bf16[1,1,128,128]{3,2,1,0:T(8,128)(2,1)} %left.1, bf16[1,1,128,128]{3,2,1,0:T(8,128)(2,1)} %right.1, s32[64]{0:T(128)} %left_sizes_in.1, s32[64]{0:T(128)} %right_sizes_in.1, s32[64]{0:T(128)} %charge_left_in.1, s32[64]{0:T(128)} %charge_right_in.1, ...), custom_call_target="tpu_custom_call" | custom-call | flops 536870912 | bytes 1048576 | tf_op jit(solution)/shard_map/pallas_call | solution.py:411
  47.4 1.7 %copy.11 = bf16[128,1024]{1,0:T(8,128)(2,1)} copy(bf16[128,1024]{1,0:T(8,128)(2,1)} %shard_map.82) | data formatting | bytes 524288

commit v7 on v5

--- a/solution.py
+++ b/solution.py
@@ -8,7 +8,7 @@
 from jax.sharding import PartitionSpec as P
 
 MESH = pl.DeviceIdType.MESH
-PIECES = 4
+PIECES = 8
 
 
 def ring_plan(nz):

time: 49.5 us -> 49.8 us (level)
  no operation moved by 1% of the time
where the time goes in v7:
time: 49.8 us; the launch traced here: 49.7 us
  Pallas kernels  47.3 us (95%)
  local copies, waits for them, and re-layouts  1.67 us (3%)
  between operations  0.66 us (1%)
    pallas_call x1, Pallas kernels, local(): pl.pallas_call(functools.partial(kernel, nx, nz, block), out_shape=jax.Sh...  47.3 us
    unnamed x1, local copies, waits for them, and re-layouts  1.67 us

profile of v7, /device:TPU:1, one launch (start us, length us, event | category | flops | bytes accessed | tf_op | source)
XLA Modules:
  0.0 49.7 jit_solution(11301888888498564660)
XLA Ops:
  0.7 47.3 %shard_map.82 = bf16[128,1024]{1,0:T(8,128)(2,1)} custom-call(bf16[128,8192]{1,0:T(8,128)(2,1)} %wave.1, bf16[1,1,128,128]{3,2,1,0:T(8,128)(2,1)} %left.1, bf16[1,1,128,128]{3,2,1,0:T(8,128)(2,1)} %right.1, s32[64]{0:T(128)} %left_sizes_in.1, s32[64]{0:T(128)} %right_sizes_in.1, s32[64]{0:T(128)} %charge_left_in.1, s32[64]{0:T(128)} %charge_right_in.1, ...), custom_call_target="tpu_custom_call" | custom-call | flops 536870912 | bytes 1048576 | tf_op jit(solution)/shard_map/pallas_call | solution.py:411
  48.0 1.7 %copy.11 = bf16[128,1024]{1,0:T(8,128)(2,1)} copy(bf16[128,1024]{1,0:T(8,128)(2,1)} %shard_map.82) | data formatting | bytes 524288
